TPU v7x, 32 devices: a whole 2x2x4 slice. The times are simulated.
32 devices in a mesh: dp: 16 (over z, x, core), tensor: 2 (over y).
Axes of the slice: x: 2, y: 2, z: 4, core: 2. Of those that a mesh axis runs over, the one named last changes fastest.
Arguments:
- tokens: bfloat16 [16, 256, 8192], P('dp', None, 'tensor'), may hold values from -6 to 6
- segment_ids: int32 [16, 256], P('dp'), may hold values from 0 to 3, never falling along the last dimension, each value on 1 to 128 neighbouring positions
- queries: bfloat16 [16, 256, 8192], P('dp', None, 'tensor'), may hold values from -7 to 7
- teacher_keys: bfloat16 [16, 256, 1024], P('dp', None, 'tensor'), may hold values from -7 to 7
- teacher_values: bfloat16 [16, 256, 1024], P('dp', None, 'tensor'), may hold values from -6 to 6
- down_weight: bfloat16 [8192, 512], P('tensor'), may hold values from -0.0625 to 0.0625
- rope_weight: bfloat16 [64, 8192], P(None, 'tensor'), may hold values from -1 to 1
- key_up: bfloat16 [512, 4096], P(None, 'tensor'), may hold values from -0.25 to 0.25
- value_up: bfloat16 [512, 8192], P(None, 'tensor'), may hold values from -0.25 to 0.25
Outputs:
- grad_down: float32 [8192, 512], P('tensor')
- grad_rope: float32 [64, 8192], P(None, 'tensor')
- grad_key_up: float32 [512, 4096], P(None, 'tensor')
- grad_value_up: float32 [512, 8192], P(None, 'tensor')
Inputs may be any that keep to these rules, and one draw needn't show every extreme that they name: `segment_ids`: along a sequence the document number never falls; each of the 4 documents holds 1 to 128 tokens, and one holds exactly 128.
All inputs are finite; a program needn't handle non-finite values.
Results may differ from a plain program's by a relative error of at most 0.011.
Values sent between devices are 32-bit elements; how exact they have to be, the bound alone decides.
A program may use at most 128 MiB of HBM per device.

v0:
```python
import functools
import math

import jax
import jax.numpy as jnp
from jax import lax
from jax.experimental import pallas as pl
from jax.experimental.pallas import tpu as pltpu
from jax.sharding import PartitionSpec as P

HEAD = 128
ROPE = 64


theta_base = 500000.0
norm_eps = 1e-06


def angle_tables(positions, width):
    half_width = width // 2
    exponent = jnp.arange(half_width, dtype=jnp.float32) * (2.0 / width)
    frequency = jnp.exp(-exponent * jnp.log(jnp.float32(theta_base)))
    angles = positions.astype(jnp.float32)[:, None] * frequency[None, :]
    return (jnp.cos(angles), jnp.sin(angles))


def rotate_last(tensor, cosine, sine_tab):
    half_width = tensor.shape[-1] // 2
    first_half = tensor[..., :half_width]
    second_half = tensor[..., half_width:]
    return jnp.concatenate(
        [
            first_half * cosine - second_half * sine_tab,
            second_half * cosine + first_half * sine_tab,
        ],
        axis=-1,
    )


def rotate_rows(matrix, cosine, sine_tab):
    half_width = matrix.shape[0] // 2
    first_half = matrix[:half_width]
    second_half = matrix[half_width:]
    return jnp.concatenate(
        [
            first_half * cosine - second_half * sine_tab,
            second_half * cosine + first_half * sine_tab,
        ],
        axis=0,
    )


def unrotate_rows(matrix, cosine, sine_tab):
    half_width = matrix.shape[0] // 2
    first_half = matrix[:half_width]
    second_half = matrix[half_width:]
    return jnp.concatenate(
        [
            first_half * cosine + second_half * sine_tab,
            second_half * cosine - first_half * sine_tab,
        ],
        axis=0,
    )


def doc_positions(segments_row):
    position_index = jnp.arange(segments_row.shape[0], dtype=jnp.int32)
    earlier = (segments_row[None, :] < segments_row[:, None]).astype(jnp.int32)
    return position_index - jnp.sum(earlier, axis=1)


def block_mask(seg_block, segments_row, row_start):
    rows_index = row_start + jnp.arange(seg_block.shape[0], dtype=jnp.int32)
    cols_index = jnp.arange(segments_row.shape[0], dtype=jnp.int32)
    return (
        (seg_block[:, None] == segments_row[None, :]) & (cols_index[None, :] <= rows_index[:, None])
    ).astype(jnp.int32)


def masked_softmax(scores, doc_mask):
    masked = jnp.where(doc_mask > 0, scores, -jnp.inf)
    peak = jnp.max(masked, axis=-1, keepdims=True)
    weights = jnp.exp(masked - peak)
    return weights / jnp.sum(weights, axis=-1, keepdims=True)


CHUNKS = 21


def sum_kernel(chunks, g_ref, out_ref, acc, from_core, from_x, result, from_mid, *sems):
    (load_s, core_s, core_r, x_s, x_r, z_s, z_r, mid_s, mid_r) = sems[:9]
    (xg_s, xg_r, own_s, own_r, fwd_s, fwd_r, keep_s) = sems[9:]
    rows = acc.shape[1] // chunks
    me = lax.axis_index("dp")
    core = lax.rem(me, 2)
    x = lax.rem(me // 2, 2)
    z = me // 4
    other_core = me + 1 - 2 * core
    other_x = me + 2 - 4 * x
    pair_z = me + 4 - 8 * lax.rem(z, 2)
    other_mid = (3 - z) * 4 + lax.rem(me, 4)
    is_mid = (z == 1) | (z == 2)
    is_end = (z == 0) | (z == 3)

    def part(k):
        return pl.ds(pl.multiple_of(k * rows, rows), rows)

    def send(src, dst, s, r, k, to):
        return pltpu.make_async_remote_copy(
            src_ref=src,
            dst_ref=dst,
            send_sem=s.at[k],
            recv_sem=r.at[k],
            device_id={"dp": to},
            device_id_type=pl.DeviceIdType.MESH,
        )

    def load(k):
        return pltpu.make_async_copy(g_ref.at[:, core, part(k)], acc.at[:, part(k)], load_s.at[k])

    def core_copy(k):
        return send(
            g_ref.at[:, 1 - core, part(k)], from_core.at[:, part(k)], core_s, core_r, k, other_core
        )

    def x_copy(k):
        return send(acc.at[1 - x, part(k)], from_x.at[part(k)], x_s, x_r, k, other_x)

    def up_copy(k):
        return send(acc.at[x, part(k)], result.at[part(k)], z_s, z_r, k, pair_z)

    def mid_copy(k):
        return send(acc.at[x, part(k)], from_mid.at[part(k)], mid_s, mid_r, k, other_mid)

    def down_copy(k):
        return send(result.at[part(k)], result.at[part(k)], z_s, z_r, k, pair_z)

    def xg_copy(k):
        return send(result.at[part(k)], out_ref.at[x, core, part(k)], xg_s, xg_r, k, other_x)

    def own_copy(k):
        return send(result.at[part(k)], out_ref.at[x, core, part(k)], own_s, own_r, k, other_core)

    def keep(k):
        return pltpu.make_async_copy(
            result.at[part(k)], out_ref.at[x, core, part(k)], keep_s.at[k]
        )

    def fwd_copy(k):
        block = out_ref.at[1 - x, core, part(k)]
        return send(block, block, fwd_s, fwd_r, k, other_core)

    barrier = pltpu.get_barrier_semaphore()
    for device in (other_core, other_x, pair_z):
        pl.semaphore_signal(
            barrier, inc=1, device_id={"dp": device}, device_id_type=pl.DeviceIdType.MESH
        )

    @pl.when(is_mid)
    def _():
        pl.semaphore_signal(
            barrier, inc=1, device_id={"dp": other_mid}, device_id_type=pl.DeviceIdType.MESH
        )
        pl.semaphore_wait(barrier, 4)

    @pl.when(is_end)
    def _():
        pl.semaphore_wait(barrier, 3)

    def stage0(k):
        load(k).start()
        core_copy(k).start()

    def stage1(k):
        load(k).wait()
        core_copy(k).wait_recv()
        acc[:, part(k), :] = acc[:, part(k), :] + from_core[:, part(k), :]
        x_copy(k).start()

    def stage2(k):
        x_copy(k).wait_recv()
        acc[x, part(k), :] = acc[x, part(k), :] + from_x[part(k), :]

        @pl.when(is_end)
        def _():
            up_copy(k).start()

    def stage3(k):
        @pl.when(is_mid)
        def _():
            up_copy(k).wait_recv()
            acc[x, part(k), :] = acc[x, part(k), :] + result[part(k), :]
            mid_copy(k).start()

    def stage4(k):
        @pl.when(is_mid)
        def _():
            mid_copy(k).wait_recv()
            result[part(k), :] = acc[x, part(k), :] + from_mid[part(k), :]
            down_copy(k).start()

    def stage5(k):
        @pl.when(is_end)
        def _():
            down_copy(k).wait_recv()

        xg_copy(k).start()
        own_copy(k).start()
        keep(k).start()

    def stage6(k):
        send(
            result.at[part(k)], out_ref.at[1 - x, core, part(k)], xg_s, xg_r, k, other_x
        ).wait_recv()
        fwd_copy(k).start()

    stages = (stage0, stage1, stage2, stage3, stage4, stage5, stage6)

    @pl.loop(0, chunks + len(stages) - 1)
    def _(t):
        for lag in reversed(range(len(stages))):
            @pl.when((t >= lag) & (t < chunks + lag))
            def _():
                stages[lag](t - lag)

    @pl.loop(0, chunks)
    def _(k):
        core_copy(k).wait_send()
        x_copy(k).wait_send()

        @pl.when(is_end)
        def _():
            up_copy(k).wait_send()

        @pl.when(is_mid)
        def _():
            mid_copy(k).wait_send()
            down_copy(k).wait_send()

        xg_copy(k).wait_send()
        own_copy(k).wait_send()
        keep(k).wait()
        fwd_copy(k).wait_send()
        send(
            result.at[part(k)], out_ref.at[x, 1 - core, part(k)], own_s, own_r, k, other_core
        ).wait_recv()
        send(
            result.at[part(k)], out_ref.at[1 - x, 1 - core, part(k)], fwd_s, fwd_r, k, other_core
        ).wait_recv()


def sum_rows(rows):
    count, width = rows.shape
    quarter = count // 4
    f32 = jnp.float32
    dma = pltpu.SemaphoreType.DMA((CHUNKS,))
    out = pl.pallas_call(
        functools.partial(sum_kernel, CHUNKS),
        out_shape=jax.ShapeDtypeStruct((2, 2, quarter, width), f32),
        in_specs=[pl.BlockSpec(memory_space=pl.ANY)],
        out_specs=pl.BlockSpec(memory_space=pl.ANY),
        scratch_shapes=[
            pltpu.VMEM((2, quarter, width), f32),
            pltpu.VMEM((2, quarter, width), f32),
            pltpu.VMEM((quarter, width), f32),
            pltpu.VMEM((quarter, width), f32),
            pltpu.VMEM((quarter, width), f32),
        ]
        + [dma] * 16,
        compiler_params=pltpu.CompilerParams(
            collective_id=0, has_side_effects=True, vmem_limit_bytes=56 * 2**20
        ),
    )(rows.reshape(2, 2, quarter, width))
    return out.reshape(count, width)


BLOCK = 512


def pack_kernel(down, kup, vup, tokens, latent_grad, rope_grad, latent, nope, value, out):
    f32 = jnp.float32
    over_tokens = (((0,), (0,)), ((), ()))
    step = pl.program_id(0)

    def columns(start):
        return pl.ds(pl.multiple_of((step - start) * BLOCK, BLOCK), BLOCK)

    @pl.when(step < down)
    def _():
        out[...] = lax.dot_general(
            tokens[:, columns(0)], latent_grad[...], over_tokens, preferred_element_type=f32
        )

    @pl.when((step >= down) & (step < down + kup))
    def _():
        out[...] = lax.dot_general(
            latent[...], nope[:, columns(down)], over_tokens, preferred_element_type=f32
        )

    @pl.when((step >= down + kup) & (step < down + kup + vup))
    def _():
        out[...] = lax.dot_general(
            latent[...], value[:, columns(down + kup)], over_tokens, preferred_element_type=f32
        )

    @pl.when(step == down + kup + vup)
    def _():
        rows = rope_grad.shape[0]
        for piece in range(down):
            out[piece * rows : (piece + 1) * rows, :] = jnp.dot(
                rope_grad[...],
                tokens[:, piece * BLOCK : (piece + 1) * BLOCK],
                preferred_element_type=f32,
            )


def unpack_kernel(down, kup, vup, total, grad_down, grad_rope, grad_kup, grad_vup):
    step = pl.program_id(0)

    @pl.when(step < down)
    def _():
        grad_down[...] = total[...]

    @pl.when((step >= down) & (step < down + kup))
    def _():
        grad_kup[...] = total[...]

    @pl.when((step >= down + kup) & (step < down + kup + vup))
    def _():
        grad_vup[...] = total[...]

    @pl.when(step == down + kup + vup)
    def _():
        rows = grad_rope.shape[0]
        for piece in range(down):
            grad_rope[:, piece * BLOCK : (piece + 1) * BLOCK] = total[
                piece * rows : (piece + 1) * rows, :
            ]


def packed_grads(tokens, latent_grad, rope_grad, latent, nope, value):
    f32 = jnp.float32
    down, kup, vup = (a.shape[1] // BLOCK for a in (tokens, nope, value))
    steps = down + kup + vup + 1
    whole = pl.BlockSpec(memory_space=pltpu.VMEM)
    params = pltpu.CompilerParams(vmem_limit_bytes=48 * 2**20)
    packed = pl.pallas_call(
        functools.partial(pack_kernel, down, kup, vup),
        grid=(steps,),
        out_shape=jax.ShapeDtypeStruct((steps * BLOCK, BLOCK), f32),
        in_specs=[whole] * 6,
        out_specs=pl.BlockSpec((BLOCK, BLOCK), lambda i: (i, 0)),
        compiler_params=params,
    )(tokens, latent_grad, rope_grad, latent, nope, value)
    total = sum_rows(packed)
    rope_rows = rope_grad.shape[0]
    return pl.pallas_call(
        functools.partial(unpack_kernel, down, kup, vup),
        grid=(steps,),
        out_shape=(
            jax.ShapeDtypeStruct((down * BLOCK, BLOCK), f32),
            jax.ShapeDtypeStruct((rope_rows, down * BLOCK), f32),
            jax.ShapeDtypeStruct((BLOCK, kup * BLOCK), f32),
            jax.ShapeDtypeStruct((BLOCK, vup * BLOCK), f32),
        ),
        in_specs=[pl.BlockSpec((BLOCK, BLOCK), lambda i: (i, 0))],
        out_specs=(
            pl.BlockSpec((BLOCK, BLOCK), lambda i: (jnp.minimum(i, down - 1), 0)),
            pl.BlockSpec((rope_rows, down * BLOCK), lambda i: (0, 0)),
            pl.BlockSpec((BLOCK, BLOCK), lambda i: (0, jnp.clip(i - down, 0, kup - 1))),
            pl.BlockSpec((BLOCK, BLOCK), lambda i: (0, jnp.clip(i - down - kup, 0, vup - 1))),
        ),
        compiler_params=params,
    )(total)


def local(
    by_kernel,
    tokens,
    segment_ids,
    queries,
    teacher_keys,
    teacher_values,
    down_weight,
    rope_weight,
    key_up,
    value_up,
):
    f32 = jnp.float32
    bf16 = jnp.bfloat16
    token_rows = tokens[0]
    segments_row = segment_ids[0]
    seq_len = token_rows.shape[0]
    heads_local = queries.shape[2] // HEAD
    kv_local = teacher_keys.shape[2] // HEAD
    group_size = heads_local // kv_local
    nope_width = HEAD - ROPE
    score_scale = 1.0 / math.sqrt(HEAD)
    contract_cols = (((1,), (1,)), ((), ()))
    contract_rows = (((0,), (0,)), ((), ()))
    positions = doc_positions(segments_row)
    cos_full, sin_full = angle_tables(positions, HEAD)
    cos_rope, sin_rope = angle_tables(positions, ROPE)
    latent_part = jnp.dot(token_rows, down_weight, preferred_element_type=f32)
    rope_part = lax.dot_general(rope_weight, token_rows, contract_cols, preferred_element_type=f32)
    latent_raw, rope_sum = lax.psum((latent_part, rope_part), "tensor")
    inv_rms = lax.rsqrt(jnp.mean(latent_raw * latent_raw, axis=-1, keepdims=True) + norm_eps)
    normed = latent_raw * inv_rms
    latent = normed.astype(bf16)
    rope_key = rotate_rows(rope_sum, cos_rope.T, sin_rope.T).astype(bf16)
    head_queries = queries[0].reshape(seq_len, heads_local, HEAD).transpose(1, 0, 2)
    teacher_q = (
        rotate_last(head_queries.astype(f32), cos_full, sin_full)
        .astype(bf16)
        .reshape(kv_local, group_size, seq_len, HEAD)
    )
    teacher_k = rotate_last(
        teacher_keys[0].reshape(seq_len, kv_local, HEAD).transpose(1, 0, 2).astype(f32),
        cos_full,
        sin_full,
    ).astype(bf16)
    teacher_v = teacher_values[0].reshape(seq_len, kv_local, HEAD).transpose(1, 0, 2)
    key_nope = (
        jnp.dot(latent, key_up, preferred_element_type=f32)
        .astype(bf16)
        .reshape(seq_len, heads_local, nope_width)
        .transpose(1, 0, 2)
    )
    head_values = (
        jnp.dot(latent, value_up, preferred_element_type=f32)
        .astype(bf16)
        .reshape(seq_len, heads_local, HEAD)
        .transpose(1, 0, 2)
    )
    rotated_q = rotate_last(head_queries[..., :ROPE].astype(f32), cos_rope, sin_rope).astype(bf16)
    student_q = jnp.concatenate([head_queries[..., ROPE:], rotated_q], axis=-1)
    student_k = jnp.concatenate(
        [key_nope, jnp.broadcast_to(rope_key.T[None], (heads_local, seq_len, ROPE))], axis=-1
    )
    block_rows = min(seq_len, 512)
    block_count = seq_len // block_rows

    def attend_block(carry, block_index):
        value_acc, key_acc = carry
        row_start = block_index * block_rows
        doc_mask = block_mask(segments_row, segments_row, row_start)
        teacher_scores = (
            jnp.einsum("kgqd,kpd->kgqp", teacher_q, teacher_k, preferred_element_type=f32)
            * score_scale
        )
        teacher_weights = masked_softmax(teacher_scores, doc_mask).astype(bf16)
        teacher_out = jnp.einsum(
            "kgqp,kpd->kgqd", teacher_weights, teacher_v, preferred_element_type=f32
        ).reshape(heads_local, block_rows, HEAD)
        student_scores = (
            jnp.einsum("hqd,hpd->hqp", student_q, student_k, preferred_element_type=f32)
            * score_scale
        )
        student_weights = masked_softmax(student_scores, doc_mask)
        student_low = student_weights.astype(bf16)
        student_out = jnp.einsum(
            "hqp,hpd->hqd", student_low, head_values, preferred_element_type=f32
        )
        out_grad = (student_out - teacher_out).astype(bf16)
        weight_grad = jnp.einsum("hqd,hpd->hqp", out_grad, head_values, preferred_element_type=f32)
        row_dot = jnp.sum(student_weights * weight_grad, axis=-1, keepdims=True)
        score_grad = (student_weights * (weight_grad - row_dot) * score_scale).astype(bf16)
        value_acc = value_acc + jnp.einsum(
            "hqp,hqd->hpd", student_low, out_grad, preferred_element_type=f32
        )
        key_acc = key_acc + jnp.einsum(
            "hqp,hqd->hpd", score_grad, student_q, preferred_element_type=f32
        )
        return ((value_acc, key_acc), None)

    zeros_acc = jnp.zeros((heads_local, seq_len, HEAD), f32)
    accums, unused = lax.scan(
        attend_block, (zeros_acc, zeros_acc), jnp.arange(block_count, dtype=jnp.int32)
    )
    value_acc, key_acc = accums
    value_flat = value_acc.astype(bf16).transpose(1, 0, 2).reshape(seq_len, heads_local * HEAD)
    nope_grad = (
        key_acc[..., :nope_width]
        .astype(bf16)
        .transpose(1, 0, 2)
        .reshape(seq_len, heads_local * nope_width)
    )
    rope_grad_part = jnp.sum(key_acc[..., nope_width:], axis=0).T
    norm_grad_part = lax.dot_general(
        nope_grad, key_up, contract_cols, preferred_element_type=f32
    ) + lax.dot_general(value_flat, value_up, contract_cols, preferred_element_type=f32)
    norm_grad, rope_grad_sum = lax.psum((norm_grad_part, rope_grad_part), "tensor")
    latent_grad = (
        (norm_grad - normed * jnp.mean(norm_grad * normed, axis=-1, keepdims=True)) * inv_rms
    ).astype(bf16)
    rope_grad = unrotate_rows(rope_grad_sum, cos_rope.T, sin_rope.T).astype(bf16)
    if by_kernel:
        return packed_grads(token_rows, latent_grad, rope_grad, latent, nope_grad, value_flat)
    grad_kup = lax.dot_general(latent, nope_grad, contract_rows, preferred_element_type=f32)
    grad_vup = lax.dot_general(latent, value_flat, contract_rows, preferred_element_type=f32)
    grad_down = lax.dot_general(token_rows, latent_grad, contract_rows, preferred_element_type=f32)
    grad_rope = jnp.dot(rope_grad, token_rows, preferred_element_type=f32)
    return lax.psum((grad_down, grad_rope, grad_kup, grad_vup), "dp")


def solution(mesh):
    in_specs = (
        P("dp", None, "tensor"),
        P("dp", None),
        P("dp", None, "tensor"),
        P("dp", None, "tensor"),
        P("dp", None, "tensor"),
        P("tensor", None),
        P(None, "tensor"),
        P(None, "tensor"),
        P(None, "tensor"),
    )
    out_specs = (P("tensor", None), P(None, "tensor"), P(None, "tensor"), P(None, "tensor"))
    by_kernel = mesh.shape["dp"] == 16 and mesh.shape["tensor"] == 2
    body = functools.partial(local, by_kernel)
    return jax.shard_map(body, mesh=mesh, in_specs=in_specs, out_specs=out_specs, check_vma=False)
```

profile of v0, /device:TPU:0, one launch (start us, length us, event | category | flops | bytes accessed | tf_op | source)
XLA Modules:
  0.0 450.0 jit_solution(3953662132492071555)
XLA Ops:
  7.2 0.0 copy-start
  7.2 0.0 all-reduce.7.cloned.1.call-start
  7.2 3.3 fusion.64
  10.5 4.9 %fusion.66 = f32[256,512]{1,0:T(8,128)} fusion(bf16[4096,512]{1,0:T(8,128)(2,1)} %param.14, bf16[1,256,4096]{2,1,0:T(8,128)(2,1)} %param.9), kind=kOutput, calls=%fused_computation.105 | convolution fusion | flops 1073741824 | bytes 6815744 | tf_op jit(solution)/shard_map/dot_general | solution.py:404
  15.4 0.0 all-reduce.7.cloned.1.call-update
  15.5 0.0 all-reduce.5.cloned.1.call-start
  15.5 0.0 copy-done.13
  15.5 0.1 convert_reduce_fusion
  15.7 0.1 convert_compare_fusion
  15.8 0.0 copy-done.11
  15.8 0.1 copy.32
  15.9 0.1 copy.33
  16.1 0.0 copy-done.12
  16.1 0.1 reshape_squeeze.8
  16.2 4.1 copy.25
  20.2 4.1 copy.26
  24.3 2.1 bitcast_convert_fusion
  26.4 0.5 multiply_cosine_fusion
  26.9 0.3 subtract_convert_fusion.2
  27.2 0.0 copy-start.3
  27.2 1.4 subtract_convert_fusion
  28.6 0.1 copy-done.3
  28.8 2.2 fusion.71
  31.0 1.6 fusion.25
  32.5 4.5 %fusion.72 = (f32[4,8,256]{2,1,0:T(8,128)S(1)}, f32[4,8,256,256]{2,3,1,0:T(8,128)}) fusion(f32[4,8,256,256]{2,3,1,0:T(8,128)S(1)} %fusion.25, pred[256,256]{0,1:T(8,128)(4,1)S(1)} %convert_compare_fusion), kind=kOutput, calls=%fused_computation.111 | output fusion | flops 12583167 | bytes 16875520 | tf_op jit(solution)/shard_map/while/body/eval_jaxpr/sub | solution.py:83
  37.1 7.2 %fusion.17 = f32[4,8,256,128]{3,2,1,0:T(8,128)} fusion(f32[4,8,256,256]{2,3,1,0:T(8,128)} %get-tuple-element.55, f32[4,8,256]{2,1,0:T(8,128)S(1)} %get-tuple-element.54, bf16[256,4,128]{2,1,0:T(4,128)(2,1)S(1)} %reshape_squeeze.8), kind=kOutput, calls=%fused_computation.27 | convolution fusion | flops 541065216 | bytes 12877824 | tf_op jit(solution)/shard_map/while/body/eval_jaxpr/kgqp,kpd->kgqd/dot_general | solution.py:452
  44.3 0.5 multiply_cosine_fusion.1
  44.8 3.5 subtract_convert_fusion.1
  48.3 0.2 all-reduce.7.cloned.1.call-done
  48.5 1.0 fusion.52
  49.5 1.2 multiply_reduce_fusion.2
  50.7 0.1 copy.29
  50.8 1.1 multiply_convert_fusion.2.latent
  52.0 1.7 convolution_convert_fusion.1
  53.7 1.5 copy.27
  55.1 1.8 copy.28
  56.9 4.9 %fusion.37 = bf16[32,32,8,128]{3,2,1,0:T(8,128)(2,1)} fusion(bf16[256,512]{1,0:T(8,128)(2,1)S(1)} %multiply_convert_fusion.2.latent, bf16[512,4096]{1,0:T(8,128)(2,1)} %param.17), kind=kOutput, calls=%fused_computation.51 | convolution fusion | flops 1074790400 | bytes 6553600 | tf_op jit(solution)/shard_map/dot_general | solution.py:430
  61.8 0.5 broadcast_in_dim.28
  62.4 3.3 fusion.21
  65.7 0.0 copy-start.10
  65.7 4.6 %fusion.73 = (f32[32,256]{1,0:T(8,128)S(1)}, f32[32,256,256]{1,2,0:T(8,128)}) fusion(f32[32,256,256]{1,2,0:T(8,128)S(1)} %fusion.21, pred[256,256]{0,1:T(8,128)(4,1)S(1)} %convert_compare_fusion), kind=kOutput, calls=%fused_computation.112 | output fusion | flops 12583167 | bytes 16875520 | tf_op jit(solution)/shard_map/while/body/eval_jaxpr/sub | solution.py:83
  70.2 6.4 %fusion.11 = bf16[32,256,128]{2,1,0:T(8,128)(2,1)S(1)} fusion(f32[4,8,256,128]{3,2,1,0:T(8,128)} %fusion.17, bf16[32,32,8,128]{3,2,1,0:T(8,128)(2,1)S(1)} %copy-done.10, f32[32,256,256]{1,2,0:T(8,128)} %get-tuple-element.57, f32[32,256]{1,0:T(8,128)S(1)} %get-tuple-element.56), kind=kOutput, calls=%fused_computation.16 | convolution fusion | flops 543162368 | bytes 16809984 | tf_op jit(solution)/shard_map/while/body/eval_jaxpr/hqp,hpd->hqd/dot_general | solution.py:461
  76.6 0.6 copy-done.14
  77.2 2.9 fusion.32
  80.1 4.7 %fusion.20 = f32[32,256,256]{1,2,0:T(8,128)} fusion(bf16[32,256,128]{2,1,0:T(8,128)(2,1)S(1)} %fusion.11, bf16[32,32,8,128]{3,2,1,0:T(8,128)(2,1)S(1)} %copy-done.10), kind=kOutput, calls=%fused_computation.32 | convolution fusion | flops 536870912 | bytes 12582912 | tf_op jit(solution)/shard_map/while/body/eval_jaxpr/hqd,hpd->hqp/dot_general | solution.py:465
  84.7 16.9 %fusion.9 = f32[32,256,128]{1,2,0:T(8,128)} fusion(f32[32,256,256]{1,2,0:T(8,128)} %fusion.20, bf16[32,256,32]{2,1,0:T(8,128)(2,1)} %get-tuple-element.29, bf16[32,256,32]{2,1,0:T(8,128)(2,1)} %get-tuple-element.28, bf16[32,256,64]{2,1,0:T(8,128)(2,1)} %get-tuple-element.42, f32[32,256,256]{1,2,0:T(8,128)} %get-tuple-element.57, ...), kind=kOutput, calls=%fused_computation.14 | convolution fusion | flops 557850880 | bytes 23101440 | tf_op jit(solution)/shard_map/while/body/eval_jaxpr/hqp,hqd->hpd/dot_general | solution.py:471
  101.6 2.5 slice_reduce_fusion
  104.1 1.7 slice.94
  105.8 0.0 copy-start.4
  105.9 3.9 fusion.74
  109.8 1.6 convolution_add_fusion
  111.3 0.0 all-reduce.5.cloned.1.call-update
  111.4 4.1 copy.50.value
  115.4 1.5 copy.41.nope
  116.9 27.4 %all-reduce.5.cloned.1.call-done = (f32[256,512]{1,0:T(8,128)}, f32[64,256]{1,0:T(8,128)}) async-done(((f32[256,512]{1,0:T(8,128)}, f32[64,256]{1,0:T(8,128)}), (f32[256,512]{1,0:T(8,128)}, f32[64,256]{1,0:T(8,128)})) %all-reduce.5.cloned.1.call-update) | async-done | bytes 589840 | tf_op jit(solution)/shard_map/psum | solution.py:492
  144.3 1.0 fusion.56
  145.3 1.4 multiply_reduce_fusion.1
  146.7 1.4 multiply_convert_fusion.1.latent_grad
  148.0 0.0 copy-start.1
  148.1 1.6 copy-done.1
  149.6 1.6 copy-done.2
  151.2 14.8 %shard_map.120 = f32[10752,512]{1,0:T(8,128)} custom-call(bf16[256,4096]{1,0:T(8,128)(2,1)S(1)} %bitcast.65, bf16[256,512]{1,0:T(8,128)(2,1)S(1)} %multiply_convert_fusion.1.latent_grad, bf16[64,256]{1,0:T(8,128)(2,1)S(1)} %pad_maximum_fusion.1.rope_grad, bf16[256,512]{1,0:T(8,128)(2,1)S(1)} %multiply_convert_fusion.2.latent, ...), custom_call_target="tpu_custom_call" | custom-call | tf_op jit(solution)/shard_map/pallas_call | solution.py:347
  166.0 253.9 %shard_map.121 = f32[2,2,2688,512]{3,2,1,0:T(8,128)} custom-call(f32[2,2,2688,512]{3,2,1,0:T(8,128)} %bitcast.66), custom_call_target="tpu_custom_call" | custom-call | tf_op jit(solution)/shard_map/pallas_call | solution.py:257
  419.9 23.3 %shard_map.122 = (f32[4096,512]{1,0:T(8,128)}, f32[64,4096]{1,0:T(8,128)}, f32[512,2048]{1,0:T(8,128)}, f32[512,4096]{1,0:T(8,128)}) custom-call(f32[10752,512]{1,0:T(8,128)} %bitcast.67), custom_call_target="tpu_custom_call" | custom-call | tf_op jit(solution)/shard_map/pallas_call | solution.py:357
  (25 shorter events, 0.1 us)
Async XLA Ops:
  7.2 44.8 %copy-start = (bf16[512,2048]{1,0:T(8,128)(2,1)S(1)}, bf16[512,2048]{1,0:T(8,128)(2,1)}, u32[]{:S(2)}) copy-start(bf16[512,2048]{1,0:T(8,128)(2,1)} %param.16) | copy-start | bytes 6291460
  7.2 41.3 %all-reduce.7.cloned.1.call-start = ((), (), s32[]{:S(2)}) async-start(), calls=%async_computation.1 | async-start | bytes 1179648 | tf_op jit(solution)/shard_map/psum | solution.py:406
  10.5 5.0 %copy-start.13 = (s32[1,256]{1,0:T(1,128)S(1)}, s32[1,256]{1,0:T(1,128)}, u32[]{:S(2)}) copy-start(s32[1,256]{1,0:T(1,128)} %param.10) | copy-start | bytes 3076
  10.5 5.3 %copy-start.11 = (bf16[1,256,512]{2,1,0:T(8,128)(2,1)S(1)}, bf16[1,256,512]{2,1,0:T(8,128)(2,1)}, u32[]{:S(2)}) copy-start(bf16[1,256,512]{2,1,0:T(8,128)(2,1)} %param.12) | copy-start | bytes 786436
  10.5 5.6 %copy-start.12 = (bf16[1,256,512]{2,1,0:T(8,128)(2,1)S(1)}, bf16[1,256,512]{2,1,0:T(8,128)(2,1)}, u32[]{:S(2)}) copy-start(bf16[1,256,512]{2,1,0:T(8,128)(2,1)} %param.13) | copy-start | bytes 786436
  15.5 128.8 %all-reduce.5.cloned.1.call-start = ((), (), s32[]{:S(2)}) async-start(), calls=%async_computation | async-start | bytes 1179648 | tf_op jit(solution)/shard_map/psum | solution.py:492
  27.2 1.6 copy-start.3
  56.9 5.4 %copy-start.5 = (bf16[32,256,64]{2,1,0:T(8,128)(2,1)S(1)}, bf16[32,256,64]{2,1,0:T(8,128)(2,1)}, u32[]{:S(2)}) copy-start(bf16[32,256,64]{2,1,0:T(8,128)(2,1)} %get-tuple-element.42) | copy-start | bytes 3145732
  56.9 5.4 %copy-start.6 = (bf16[32,256,32]{2,1,0:T(8,128)(2,1)S(1)}, bf16[32,256,32]{2,1,0:T(8,128)(2,1)}, u32[]{:S(2)}) copy-start(bf16[32,256,32]{2,1,0:T(8,128)(2,1)} %get-tuple-element.28) | copy-start | bytes 1572868
  56.9 5.4 %copy-start.7 = (bf16[32,256,32]{2,1,0:T(8,128)(2,1)S(1)}, bf16[32,256,32]{2,1,0:T(8,128)(2,1)}, u32[]{:S(2)}) copy-start(bf16[32,256,32]{2,1,0:T(8,128)(2,1)} %get-tuple-element.29) | copy-start | bytes 1572868
  56.9 5.4 %copy-start.8 = (bf16[256,32,64]{2,0,1:T(8,128)(2,1)S(1)}, bf16[256,32,64]{2,0,1:T(8,128)(2,1)}, u32[]{:S(2)}) copy-start(bf16[256,32,64]{2,0,1:T(8,128)(2,1)} %copy.28) | copy-start | bytes 3145732
  65.7 4.6 %copy-start.10 = (bf16[32,32,8,128]{3,2,1,0:T(8,128)(2,1)S(1)}, bf16[32,32,8,128]{3,2,1,0:T(8,128)(2,1)}, u32[]{:S(2)}) copy-start(bf16[32,32,8,128]{3,2,1,0:T(8,128)(2,1)} %fusion.37) | copy-start | bytes 6291460
  70.2 7.0 %copy-start.14 = (f32[32,256,256]{1,2,0:T(8,128)S(1)}, f32[32,256,256]{1,2,0:T(8,128)}, u32[]{:S(2)}) copy-start(f32[32,256,256]{1,2,0:T(8,128)} %get-tuple-element.57) | copy-start | bytes 25165828
  101.6 4.2 copy-start.9
  105.8 5.5 %copy-start.4 = (bf16[32,256,64]{1,2,0:T(8,128)(2,1)}, bf16[32,256,64]{1,2,0:T(8,128)(2,1)S(1)}, u32[]{:S(2)}) copy-start(bf16[32,256,64]{1,2,0:T(8,128)(2,1)S(1)} %slice.94) | copy-start | bytes 3145732
  148.0 1.6 copy-start.1
  149.6 1.6 copy-start.2
Sparse Core Ops, SparseCore 0:
  15.6 32.9 all-reduce.6
  111.5 32.7 all-reduce.4
where the time goes:
time: 452 us; the launch traced here: 450 us
  Pallas kernels  292 us (65%)
  matrix products  63.1 us (14%)
  other arithmetic  29.4 us (7%)
  waiting for transfers between devices  27.6 us (6%)
  local copies, waits for them, and re-layouts  23.5 us (5%)
  between operations  14.4 us (3%)
    pallas_call x1, Pallas kernels, sum_rows(): pl.pallas_call(functools.partial(sum_kernel, CHUNKS), out_shape=jax.Shape...  254 us
    psum x1, waiting for transfers between devices, local(): lax.psum((norm_grad_part, rope_grad_part), 'tensor')  27.4 us
    pallas_call x1, Pallas kernels, packed_grads(): pl.pallas_call(functools.partial(unpack_kernel, down, kup, vup), grid=(st...  23.3 us
    dot_general x1, matrix products, attend_block(): jnp.einsum('hqp,hqd->hpd', score_grad, student_q, preferred_element_type=...  16.9 us
    pallas_call x1, Pallas kernels, packed_grads(): pl.pallas_call(functools.partial(pack_kernel, down, kup, vup), grid=(step...  14.8 us
    sub x2, other arithmetic, masked_softmax(): weights = jnp.exp(masked - peak)  9.09 us
  transfers between devices with their start and end apart: 2, of which 2 were waited for; matrix products, arithmetic and copies ran while one was open for 8% of the time, Pallas kernels for 0%

commit v1 on v0

--- a/solution.py
+++ b/solution.py
@@ -374,6 +374,12 @@
     )(total)
 
 
+def tensor_sum(parts, is_pair):
+    if not is_pair:
+        return lax.psum(parts, "tensor")
+    return tuple(part + lax.ppermute(part, "tensor", ((0, 1), (1, 0))) for part in parts)
+
+
 def local(
     by_kernel,
     tokens,
@@ -403,7 +409,7 @@
     cos_rope, sin_rope = angle_tables(positions, ROPE)
     latent_part = jnp.dot(token_rows, down_weight, preferred_element_type=f32)
     rope_part = lax.dot_general(rope_weight, token_rows, contract_cols, preferred_element_type=f32)
-    latent_raw, rope_sum = lax.psum((latent_part, rope_part), "tensor")
+    latent_raw, rope_sum = tensor_sum((latent_part, rope_part), by_kernel)
     inv_rms = lax.rsqrt(jnp.mean(latent_raw * latent_raw, axis=-1, keepdims=True) + norm_eps)
     normed = latent_raw * inv_rms
     latent = normed.astype(bf16)
@@ -489,7 +495,7 @@
     norm_grad_part = lax.dot_general(
         nope_grad, key_up, contract_cols, preferred_element_type=f32
     ) + lax.dot_general(value_flat, value_up, contract_cols, preferred_element_type=f32)
-    norm_grad, rope_grad_sum = lax.psum((norm_grad_part, rope_grad_part), "tensor")
+    norm_grad, rope_grad_sum = tensor_sum((norm_grad_part, rope_grad_part), by_kernel)
     latent_grad = (
         (norm_grad - normed * jnp.mean(norm_grad * normed, axis=-1, keepdims=True)) * inv_rms
     ).astype(bf16)

time: 452 us -> 425 us (0.940)
  waiting for transfers between devices: 27.6 us -> 12.7 us
  between operations: 14.4 us -> 1.03 us
  starting transfers between devices: 0.08 us -> 5.26 us
    psum x2 -> x0, waiting for transfers between devices: 27.6 us -> none  [the longest x1 27.4 us: local(): lax.psum((norm_grad_part, rope_grad_part), 'tensor')]
    ppermute x0 -> x4, waiting for transfers between devices: none -> 12.7 us  [tensor_sum(): lax.ppermute(part, 'tensor', ((0, 1), (1, 0)))]
    ppermute x0 -> x4, starting transfers between devices: none -> 5.26 us  [tensor_sum(): lax.ppermute(part, 'tensor', ((0, 1), (1, 0)))]
  transfers between devices with their start and end apart: 2 -> 4, of which waited for: 2 -> 1; matrix products, arithmetic and copies ran while one was open for 8% -> 11% of each run, Pallas kernels for 0% -> 0%
where the time goes in v1:
time: 425 us; the launch traced here: 423 us
  Pallas kernels  292 us (69%)
  matrix products  62.5 us (15%)
  other arithmetic  26.9 us (6%)
  local copies, waits for them, and re-layouts  22.9 us (5%)
  waiting for transfers between devices  12.7 us (3%)
  starting transfers between devices  5.26 us (1%)
    pallas_call x1, Pallas kernels, sum_rows(): pl.pallas_call(functools.partial(sum_kernel, CHUNKS), out_shape=jax.Shape...  254 us
    pallas_call x1, Pallas kernels, packed_grads(): pl.pallas_call(functools.partial(unpack_kernel, down, kup, vup), grid=(st...  23.3 us
    dot_general x1, matrix products, attend_block(): jnp.einsum('hqp,hqd->hpd', score_grad, student_q, preferred_element_type=...  17 us
    pallas_call x1, Pallas kernels, packed_grads(): pl.pallas_call(functools.partial(pack_kernel, down, kup, vup), grid=(step...  14.7 us
    ppermute x4, waiting for transfers between devices, tensor_sum(): lax.ppermute(part, 'tensor', ((0, 1), (1, 0)))  12.7 us
    sub x2, other arithmetic, masked_softmax(): weights = jnp.exp(masked - peak)  9.09 us
  transfers between devices with their start and end apart: 4, of which 1 were waited for; matrix products, arithmetic and copies ran while one was open for 11% of the time, Pallas kernels for 0%

profile of v1, /device:TPU:0, one launch (start us, length us, event | category | flops | bytes accessed | tf_op | source)
XLA Modules:
  0.0 423.5 jit_solution(17548955672062372889)
XLA Ops:
  0.6 0.0 copy-start
  0.6 2.7 fusion.64
  3.3 0.0 copy-start.16
  3.3 0.0 copy-start.12
  3.3 0.0 copy-start.13
  3.3 3.0 collective-permute-start.1
  6.4 4.9 %fusion.66 = f32[256,512]{1,0:T(8,128)} fusion(bf16[4096,512]{1,0:T(8,128)(2,1)} %param.14, bf16[1,256,4096]{2,1,0:T(8,128)(2,1)} %param.9), kind=kOutput, calls=%fused_computation.106 | convolution fusion | flops 1073741824 | bytes 6815744 | tf_op jit(solution)/shard_map/dot_general | solution.py:410
  11.2 0.1 collective-permute-start
  11.3 0.1 convert_reduce_fusion
  11.5 0.7 convert_compare_fusion
  12.2 0.1 copy.32
  12.3 0.1 copy.33
  12.5 0.1 reshape_squeeze.8
  12.5 0.5 multiply_cosine_fusion
  13.1 0.5 multiply_cosine_fusion.1
  13.6 4.3 %copy.25 = bf16[1,256,4096]{1,2,0:T(8,128)(2,1)} copy(bf16[1,256,4096]{2,1,0:T(8,128)(2,1)} %param.11) | data formatting | bytes 4194304 | tf_op args[2]
  17.9 4.1 copy.26
  21.9 2.1 bitcast_convert_fusion
  24.0 0.3 subtract_convert_fusion.2
  24.3 0.0 copy-start.3
  24.3 1.4 subtract_convert_fusion
  25.8 0.1 copy-done.3
  25.9 2.2 fusion.71
  28.1 1.6 fusion.25
  29.7 4.5 %fusion.72 = (f32[4,8,256]{2,1,0:T(8,128)S(1)}, f32[4,8,256,256]{2,3,1,0:T(8,128)}) fusion(f32[4,8,256,256]{2,3,1,0:T(8,128)S(1)} %fusion.25, pred[256,256]{0,1:T(8,128)(4,1)S(1)} %copy-done.14), kind=kOutput, calls=%fused_computation.112 | output fusion | flops 12583167 | bytes 16875520 | tf_op jit(solution)/shard_map/while/body/eval_jaxpr/sub | solution.py:83
  34.2 7.1 %fusion.17 = f32[4,8,256,128]{3,2,1,0:T(8,128)} fusion(f32[4,8,256,256]{2,3,1,0:T(8,128)} %get-tuple-element.55, f32[4,8,256]{2,1,0:T(8,128)S(1)} %get-tuple-element.54, bf16[256,4,128]{2,1,0:T(4,128)(2,1)S(1)} %reshape_squeeze.8), kind=kOutput, calls=%fused_computation.27 | convolution fusion | flops 541065216 | bytes 12877824 | tf_op jit(solution)/shard_map/while/body/eval_jaxpr/kgqp,kpd->kgqd/dot_general | solution.py:458
  41.3 3.5 subtract_convert_fusion.1
  44.8 0.2 fusion.52
  45.1 0.1 copy.29
  45.2 1.3 multiply_reduce_fusion.2
  46.5 0.8 copy-done.9
  47.4 0.1 multiply_convert_fusion.2.latent
  47.5 1.7 convolution_convert_fusion.1
  49.2 1.5 copy.27
  50.6 1.8 copy.28
  52.4 4.9 %fusion.37 = bf16[32,32,8,128]{3,2,1,0:T(8,128)(2,1)} fusion(bf16[256,512]{1,0:T(8,128)(2,1)S(1)} %multiply_convert_fusion.2.latent, bf16[512,4096]{1,0:T(8,128)(2,1)} %param.17), kind=kOutput, calls=%fused_computation.51 | convolution fusion | flops 1074790400 | bytes 6553600 | tf_op jit(solution)/shard_map/dot_general | solution.py:436
  57.4 0.5 broadcast_in_dim.28
  57.9 3.3 fusion.21
  61.2 0.0 copy-start.11
  61.2 4.6 %fusion.73 = (f32[32,256]{1,0:T(8,128)S(1)}, f32[32,256,256]{1,2,0:T(8,128)}) fusion(f32[32,256,256]{1,2,0:T(8,128)S(1)} %fusion.21, pred[256,256]{0,1:T(8,128)(4,1)S(1)} %copy-done.15), kind=kOutput, calls=%fused_computation.113 | output fusion | flops 12583167 | bytes 16875520 | tf_op jit(solution)/shard_map/while/body/eval_jaxpr/sub | solution.py:83
  65.8 6.4 %fusion.11 = bf16[32,256,128]{2,1,0:T(8,128)(2,1)S(1)} fusion(f32[4,8,256,128]{3,2,1,0:T(8,128)} %fusion.17, bf16[32,32,8,128]{3,2,1,0:T(8,128)(2,1)S(1)} %copy-done.11, f32[32,256,256]{1,2,0:T(8,128)} %get-tuple-element.57, f32[32,256]{1,0:T(8,128)S(1)} %get-tuple-element.56), kind=kOutput, calls=%fused_computation.16 | convolution fusion | flops 543162368 | bytes 16809984 | tf_op jit(solution)/shard_map/while/body/eval_jaxpr/hqp,hpd->hqd/dot_general | solution.py:467
  72.1 0.6 copy-done.17
  72.7 2.9 fusion.32
  75.6 4.7 %fusion.20 = f32[32,256,256]{1,2,0:T(8,128)} fusion(bf16[32,256,128]{2,1,0:T(8,128)(2,1)S(1)} %fusion.11, bf16[32,32,8,128]{3,2,1,0:T(8,128)(2,1)S(1)} %copy-done.11), kind=kOutput, calls=%fused_computation.32 | convolution fusion | flops 536870912 | bytes 12582912 | tf_op jit(solution)/shard_map/while/body/eval_jaxpr/hqd,hpd->hqp/dot_general | solution.py:471
  80.3 17.0 %fusion.9 = f32[32,256,128]{1,2,0:T(8,128)} fusion(f32[32,256,256]{1,2,0:T(8,128)} %fusion.20, bf16[32,256,32]{2,1,0:T(8,128)(2,1)} %get-tuple-element.29, bf16[32,256,32]{2,1,0:T(8,128)(2,1)} %get-tuple-element.28, bf16[32,256,64]{2,1,0:T(8,128)(2,1)} %get-tuple-element.42, f32[32,256,256]{1,2,0:T(8,128)} %get-tuple-element.57, ...), kind=kOutput, calls=%fused_computation.14 | convolution fusion | flops 557850880 | bytes 23101440 | tf_op jit(solution)/shard_map/while/body/eval_jaxpr/hqp,hqd->hpd/dot_general | solution.py:477
  97.3 1.9 slice_reduce_fusion
  99.2 1.7 slice.94
  100.9 0.0 copy-start.4
  100.9 3.9 fusion.74
  104.9 2.0 collective-permute-start.3
  106.9 1.6 convolution_add_fusion
  108.4 4.1 copy.50.value
  112.5 1.5 copy.41.nope
  114.0 0.0 copy-start.1
  114.0 0.1 collective-permute-start.2
  114.2 0.2 fusion.56
  114.4 12.7 %collective-permute-done.2 = f32[256,512]{1,0:T(8,128)S(1)} collective-permute-done((f32[256,512]{1,0:T(8,128)}, f32[256,512]{1,0:T(8,128)S(1)}, u32[]{:S(2)}, u32[]{:S(2)}) %collective-permute-start.2) | collective-permute-done | bytes 524320 | tf_op jit(solution)/shard_map/ppermute | solution.py:380
  127.1 1.4 multiply_reduce_fusion.1
  128.5 1.2 multiply_convert_fusion.1.latent_grad
  129.7 0.0 copy-start.2
  129.7 1.6 copy-done.2
  131.3 14.7 %shard_map.120 = f32[10752,512]{1,0:T(8,128)} custom-call(bf16[256,4096]{1,0:T(8,128)(2,1)S(1)} %bitcast.66, bf16[256,512]{1,0:T(8,128)(2,1)S(1)} %multiply_convert_fusion.1.latent_grad, bf16[64,256]{1,0:T(8,128)(2,1)S(1)} %pad_maximum_fusion.1.rope_grad, bf16[256,512]{1,0:T(8,128)(2,1)S(1)} %multiply_convert_fusion.2.latent, ...), custom_call_target="tpu_custom_call" | custom-call | tf_op jit(solution)/shard_map/pallas_call | solution.py:347
  146.0 254.2 %shard_map.121 = f32[2,2,2688,512]{3,2,1,0:T(8,128)} custom-call(f32[2,2,2688,512]{3,2,1,0:T(8,128)} %bitcast.67), custom_call_target="tpu_custom_call" | custom-call | tf_op jit(solution)/shard_map/pallas_call | solution.py:257
  400.2 23.3 %shard_map.122 = (f32[4096,512]{1,0:T(8,128)}, f32[64,4096]{1,0:T(8,128)}, f32[512,2048]{1,0:T(8,128)}, f32[512,4096]{1,0:T(8,128)}) custom-call(f32[10752,512]{1,0:T(8,128)} %bitcast.68), custom_call_target="tpu_custom_call" | custom-call | tf_op jit(solution)/shard_map/pallas_call | solution.py:357
  (35 shorter events, 0.1 us)
Async XLA Ops:
  0.6 46.8 %copy-start = (bf16[512,2048]{1,0:T(8,128)(2,1)S(1)}, bf16[512,2048]{1,0:T(8,128)(2,1)}, u32[]{:S(2)}) copy-start(bf16[512,2048]{1,0:T(8,128)(2,1)} %param.16) | copy-start | bytes 6291460
  3.3 8.0 %copy-start.16 = (s32[1,256]{1,0:T(1,128)S(1)}, s32[1,256]{1,0:T(1,128)}, u32[]{:S(2)}) copy-start(s32[1,256]{1,0:T(1,128)} %param.10) | copy-start | bytes 3076
  3.3 8.9 %copy-start.12 = (bf16[1,256,512]{2,1,0:T(8,128)(2,1)S(1)}, bf16[1,256,512]{2,1,0:T(8,128)(2,1)}, u32[]{:S(2)}) copy-start(bf16[1,256,512]{2,1,0:T(8,128)(2,1)} %param.12) | copy-start | bytes 786436
  3.3 9.1 %copy-start.13 = (bf16[1,256,512]{2,1,0:T(8,128)(2,1)S(1)}, bf16[1,256,512]{2,1,0:T(8,128)(2,1)}, u32[]{:S(2)}) copy-start(bf16[1,256,512]{2,1,0:T(8,128)(2,1)} %param.13) | copy-start | bytes 786436
  3.3 41.5 %collective-permute-start.1 = (f32[64,256]{1,0:T(8,128)S(1)}, f32[64,256]{1,0:T(8,128)S(1)}, u32[]{:S(2)}, u32[]{:S(2)}) collective-permute-start(f32[64,256]{1,0:T(8,128)S(1)} %fusion.64), channel_id=1, source_target_pairs={{0,1},{1,0},{2,3},{3,2},{4,5},{5,4},{6,7},{7,6},{8,9},{9,8},{10,11... | collective-permute-start | bytes 196616 | tf_op jit(solution)/shard_map/ppermute | solution.py:380
  11.2 33.9 %collective-permute-start = (f32[256,512]{1,0:T(8,128)}, f32[256,512]{1,0:T(8,128)}, u32[]{:S(2)}, u32[]{:S(2)}) collective-permute-start(f32[256,512]{1,0:T(8,128)} %fusion.66), channel_id=1, source_target_pairs={{0,1},{1,0},{2,3},{3,2},{4,5},{5,4},{6,7},{7,6},{8,9},{9,8},{10,11... | collective-permute-start | bytes 1572872 | tf_op jit(solution)/shard_map/ppermute | solution.py:380
  24.3 1.6 copy-start.3
  28.1 1.6 copy-start.14
  46.5 0.8 copy-start.9
  52.4 5.4 %copy-start.5 = (bf16[32,256,64]{2,1,0:T(8,128)(2,1)S(1)}, bf16[32,256,64]{2,1,0:T(8,128)(2,1)}, u32[]{:S(2)}) copy-start(bf16[32,256,64]{2,1,0:T(8,128)(2,1)} %get-tuple-element.42) | copy-start | bytes 3145732
  52.4 5.4 %copy-start.6 = (bf16[32,256,32]{2,1,0:T(8,128)(2,1)S(1)}, bf16[32,256,32]{2,1,0:T(8,128)(2,1)}, u32[]{:S(2)}) copy-start(bf16[32,256,32]{2,1,0:T(8,128)(2,1)} %get-tuple-element.28) | copy-start | bytes 1572868
  52.4 5.4 %copy-start.7 = (bf16[32,256,32]{2,1,0:T(8,128)(2,1)S(1)}, bf16[32,256,32]{2,1,0:T(8,128)(2,1)}, u32[]{:S(2)}) copy-start(bf16[32,256,32]{2,1,0:T(8,128)(2,1)} %get-tuple-element.29) | copy-start | bytes 1572868
  52.4 5.4 %copy-start.8 = (bf16[256,32,64]{2,0,1:T(8,128)(2,1)S(1)}, bf16[256,32,64]{2,0,1:T(8,128)(2,1)}, u32[]{:S(2)}) copy-start(bf16[256,32,64]{2,0,1:T(8,128)(2,1)} %copy.28) | copy-start | bytes 3145732
  57.9 3.3 copy-start.15
  61.2 4.6 %copy-start.11 = (bf16[32,32,8,128]{3,2,1,0:T(8,128)(2,1)S(1)}, bf16[32,32,8,128]{3,2,1,0:T(8,128)(2,1)}, u32[]{:S(2)}) copy-start(bf16[32,32,8,128]{3,2,1,0:T(8,128)(2,1)} %fusion.37) | copy-start | bytes 6291460
  65.8 7.0 %copy-start.17 = (f32[32,256,256]{1,2,0:T(8,128)S(1)}, f32[32,256,256]{1,2,0:T(8,128)}, u32[]{:S(2)}) copy-start(f32[32,256,256]{1,2,0:T(8,128)} %get-tuple-element.57) | copy-start | bytes 25165828
  97.3 3.6 copy-start.10
  100.9 5.9 %copy-start.4 = (bf16[32,256,64]{1,2,0:T(8,128)(2,1)}, bf16[32,256,64]{1,2,0:T(8,128)(2,1)S(1)}, u32[]{:S(2)}) copy-start(bf16[32,256,64]{1,2,0:T(8,128)(2,1)S(1)} %slice.94) | copy-start | bytes 3145732
  104.9 9.3 %collective-permute-start.3 = (f32[64,256]{1,0:T(8,128)S(1)}, f32[64,256]{1,0:T(8,128)S(1)}, u32[]{:S(2)}, u32[]{:S(2)}) collective-permute-start(f32[64,256]{1,0:T(8,128)S(1)} %bitcast.81), channel_id=1, source_target_pairs={{0,1},{1,0},{2,3},{3,2},{4,5},{5,4},{6,7},{7,6},{8,9},{9,8},{10,11... | collective-permute-start | bytes 196616 | tf_op jit(solution)/shard_map/ppermute | solution.py:380
  114.0 15.7 %copy-start.1 = (bf16[1,256,4096]{2,1,0:T(8,128)(2,1)S(1)}, bf16[1,256,4096]{2,1,0:T(8,128)(2,1)}, u32[]{:S(2)}) copy-start(bf16[1,256,4096]{2,1,0:T(8,128)(2,1)} %param.9) | copy-start | bytes 6291460
  114.0 13.1 %collective-permute-start.2 = (f32[256,512]{1,0:T(8,128)}, f32[256,512]{1,0:T(8,128)S(1)}, u32[]{:S(2)}, u32[]{:S(2)}) collective-permute-start(f32[256,512]{1,0:T(8,128)} %convolution_add_fusion), channel_id=1, source_target_pairs={{0,1},{1,0},{2,3},{3,2},{4,5},{5,4},{6,7},{7,6},{8,9},{9,8},{10,11... | collective-permute-start | bytes 1572872 | tf_op jit(solution)/shard_map/ppermute | solution.py:380
  129.7 1.6 copy-start.2
